TPU v7x, 32 devices: a whole 2x2x4 slice. The times are simulated.
32 devices in a mesh: band: 16 (over z, y, x), shell: 2 (over core).
Axes of the slice: x: 2, y: 2, z: 4, core: 2. Of those that a mesh axis runs over, the one named last changes fastest.
Arguments:
- spectrum: float32 [2, 3, 2, 512, 512], P('shell', None, None, 'band'), parts along dimension 0, may hold values from -6 to 6
- capture_rate: float32 [2, 1024, 2048], P('shell', 'band'), parts along dimension 0, may hold values from 0.5 to 1500, as said below
- row_latitude: int32 [1024], replicated, may hold values from 0 to 1023, each once
- slot_wavenumber: int32 [512], replicated, may hold values from 0 to 511, each once
Outputs:
- transport: float32 [2, 3, 2, 512, 512], P('shell', None, None, 'band'), parts along dimension 0
There are 2 independent parts, one for each index of `shell`. A program takes and returns all parts, laid end to end along the dimension named above; an argument that names none is the same for every part. Nothing has to cross between parts.
Inputs may be any that keep to these rules, and one draw needn't show every extreme that they name: `row_latitude`: each latitude index appears once. `slot_wavenumber`: each wavenumber appears once. `capture_rate`: positive.
All inputs are finite; a program needn't handle non-finite values.
Results may differ from a plain program's by a relative error of at most 0.0013.
Values sent between devices are 32-bit elements; how exact they have to be, the bound alone decides.
No kernel may reach another device: no remote copies, remote signals or barrier semaphores. Data moves between devices by JAX's collectives and lax.ppermute only.
A program may use at most 128 MiB of HBM per device.

v0:
```python
import math

import jax
import jax.numpy as jnp
from jax import lax
from jax.sharding import PartitionSpec as P

DEG = 512
NLAT = 1024
NLON = 2048
FIELDS = 3


LOG_LARGE = 60.0 * math.log(2.0)


def legendre_halves(orders, cosine, log_sine, degree_count):
    order_float = orders.astype(jnp.float32)[:, None]
    indices = jnp.arange(1, degree_count, dtype=jnp.float32)
    log_terms = jnp.where(
        indices[None, :] <= order_float,
        0.5 * jnp.log((2.0 * indices + 1.0) / (2.0 * indices))[None, :],
        jnp.float32(0.0),
    )
    log_norm = jnp.where(
        order_float > 0,
        0.5 * math.log(2.0) + jnp.sum(log_terms, axis=1, keepdims=True),
        jnp.float32(0.0),
    )
    start_log = log_norm + order_float * log_sine[None, :]
    cos_row = cosine[None, :]
    order_sq = order_float * order_float

    def one_degree(carry, degree):
        current, previous, log_scale = carry
        denominator = degree * degree - order_sq
        safe_denom = jnp.where(denominator > 0, denominator, jnp.float32(1.0))
        alpha_coef = jnp.sqrt((4.0 * degree * degree - 1.0) / safe_denom)
        back_term = jnp.maximum((degree - 1.0) * (degree - 1.0) - order_sq, 0.0)
        beta_coef = jnp.sqrt(
            back_term * (2.0 * degree + 1.0) / (safe_denom * jnp.maximum(2.0 * degree - 3.0, 1.0))
        )
        recursed = alpha_coef * cos_row * current - beta_coef * previous
        newest = jnp.where(
            degree > order_float,
            recursed,
            jnp.where(degree == order_float, jnp.float32(1.0), jnp.float32(0.0)),
        )
        too_large = jnp.abs(newest) > 2.0**60
        newest = jnp.where(too_large, newest * 2.0 ** (-60), newest)
        older = jnp.where(too_large, current * 2.0 ** (-60), current)
        log_scale = jnp.where(too_large, log_scale + LOG_LARGE, log_scale)
        return ((newest, older, log_scale), newest * jnp.exp(log_scale))

    def two_degrees(carry, step_index):
        degree = 2.0 * step_index
        carry, even_value = one_degree(carry, degree)
        carry, odd_value = one_degree(carry, degree + 1.0)
        return (carry, (even_value, odd_value))

    zeros_start = jnp.zeros_like(start_log)
    steps = jnp.arange(degree_count // 2, dtype=jnp.float32)
    unused, tables = lax.scan(two_degrees, (zeros_start, zeros_start, start_log), steps, unroll=16)
    return tables


def unfold(even_sum, odd_sum, parity_sign):
    northern = even_sum + odd_sum
    southern = parity_sign[None, :, None] * (even_sum - odd_sum)
    return jnp.concatenate([northern, jnp.flip(southern, -1)], -1)


def fold(by_latitude, parity_sign):
    half_lat = by_latitude.shape[-1] // 2
    northern = by_latitude[..., :half_lat]
    southern = jnp.flip(by_latitude[..., half_lat:], -1) * parity_sign[None, :, None]
    return (northern + southern, northern - southern)


def alternate(even_out, odd_out):
    channels, orders_here, half_deg = even_out.shape
    return jnp.stack([even_out, odd_out], -1).reshape(channels, orders_here, 2 * half_deg)


def synthesize(coeffs, even_table, odd_table, parity_sign):
    even_sum = jnp.einsum(
        "kmj,cmk->cmj", even_table, coeffs[:, :, 0::2], precision=lax.Precision.HIGHEST
    )
    odd_sum = jnp.einsum(
        "kmj,cmk->cmj", odd_table, coeffs[:, :, 1::2], precision=lax.Precision.HIGHEST
    )
    return unfold(even_sum, odd_sum, parity_sign)


def analyze(by_latitude, even_table, odd_table, parity_sign):
    even_data, odd_data = fold(by_latitude, parity_sign)
    even_out = jnp.einsum("kmj,cmj->cmk", even_table, even_data, precision=lax.Precision.HIGHEST)
    odd_out = jnp.einsum("kmj,cmj->cmk", odd_table, odd_data, precision=lax.Precision.HIGHEST)
    return alternate(even_out, odd_out)


def per_device(spectrum, capture_rate, row_latitude, slot_wavenumber):
    shells = spectrum.shape[0]
    local_modes = spectrum.shape[3]
    row_count = capture_rate.shape[1]
    channels = shells * FIELDS * 2
    band_index = lax.axis_index("band")
    half_lat = NLAT // 2
    north_theta = jnp.pi * (jnp.arange(half_lat, dtype=jnp.float32) + 0.5) / NLAT
    cosine = jnp.cos(north_theta)
    log_sine = jnp.log(jnp.sin(north_theta))
    local_orders = lax.dynamic_slice_in_dim(slot_wavenumber, band_index * local_modes, local_modes)
    parity_sign = (1 - 2 * (local_orders % 2)).astype(jnp.float32)
    even_table, odd_table = legendre_halves(local_orders, cosine, log_sine, DEG)
    coeffs = spectrum.reshape(channels, local_modes, DEG)
    lat_values = synthesize(coeffs, even_table, odd_table, parity_sign)
    row_values = jnp.take(lat_values, row_latitude, axis=2).reshape(
        shells, FIELDS, 2, local_modes, NLAT
    )
    longitudes = jnp.arange(NLON, dtype=jnp.int32)
    phase_index = slot_wavenumber[:, None] * longitudes[None, :] % NLON
    phase_angle = phase_index.astype(jnp.float32) * (2.0 * math.pi / NLON)
    cos_tab = jnp.cos(phase_angle)
    sin_tab = jnp.sin(phase_angle)
    block_data = lax.all_to_all(row_values, "band", split_axis=4, concat_axis=3, tiled=True)
    grid_fields = (
        jnp.einsum("sfmr,mk->sfrk", block_data[:, :, 0], cos_tab, precision=lax.Precision.HIGHEST)
        + jnp.einsum("sfmr,mk->sfrk", block_data[:, :, 1], sin_tab, precision=lax.Precision.HIGHEST)
    ) / DEG
    my_latitudes = lax.dynamic_slice_in_dim(row_latitude, band_index * row_count, row_count)
    row_sine = jnp.sin(jnp.pi * (my_latitudes.astype(jnp.float32) + 0.5) / NLAT)
    local_total = jnp.sum(capture_rate * row_sine[None, :, None], axis=(1, 2)) * (
        math.pi / (2.0 * NLAT * NLON)
    )
    concentration = grid_fields[:, 0]
    row_weight = DEG * math.pi * row_sine / (2.0 * NLAT * NLON)
    lat_to_row = jnp.argsort(row_latitude)
    rate_mean = lax.psum(local_total, "band")
    sink_term = capture_rate * concentration / rate_mean[:, None, None]
    products = jnp.stack(
        [grid_fields[:, 1] * concentration, grid_fields[:, 2] * concentration, sink_term], 1
    )
    weighted = products * row_weight[None, None, :, None]
    transforms = jnp.stack(
        [
            jnp.einsum("sfrk,mk->sfmr", weighted, cos_tab, precision=lax.Precision.HIGHEST),
            jnp.einsum("sfrk,mk->sfmr", weighted, sin_tab, precision=lax.Precision.HIGHEST),
        ],
        2,
    )
    block_data = lax.all_to_all(transforms, "band", split_axis=3, concat_axis=4, tiled=True)
    item_count = block_data.shape[0]
    ordered = jnp.take(block_data, lat_to_row, axis=4).reshape(
        item_count * FIELDS * 2, local_modes, NLAT
    )
    result = analyze(ordered, even_table, odd_table, parity_sign)
    return result.reshape(item_count, FIELDS, 2, local_modes, DEG)


def solution(mesh):
    return jax.shard_map(
        per_device,
        mesh=mesh,
        in_specs=(P("shell", None, None, "band", None), P("shell", "band", None), P(), P()),
        out_specs=P("shell", None, None, "band", None),
        check_vma=False,
    )
```

profile of v0, /device:TPU:0, one launch (start us, length us, event | category | flops | bytes accessed | tf_op | source)
XLA Modules:
  0.0 1097.1 jit_solution(1062487564874718981)
XLA Ops:
  1.6 7.5 slice.204
  9.2 7.5 slice.203
  18.4 762.2 %while.25 = (s32[]{:T(128)}, f32[32,512]{1,0:T(8,128)S(1)}, f32[32,512]{1,0:T(8,128)S(1)}, f32[32,512]{1,0:T(8,128)S(1)}, f32[16,16,32,512]{3,2,1,0:T(8,128)}, /...) while((s32[]{:T(128)}, f32[32,512]{1,0:T(8,128)S(1)}, ...), condition=%wide.region_3.4_spmd.clone.clone, body=%wide.region_2.3_spmd.clone.clone.sunk | while | flops 14237697 | bytes 12877520 | solution.py:63
  397.6 1.8 bitcast_dynamic-update-slice_fusion.3
  445.4 1.8 bitcast_dynamic-update-slice_fusion.3
  780.6 24.1 %fusion.163 = f32[32,512,6]{1,2,0:T(8,128)S(1)} fusion(f32[256,32,512]{2,1,0:T(8,128)} %bitcast.931, f32[6,32,256]{2,1,0:T(8,128)S(1)} %slice.204), kind=kOutput, calls=%fused_computation.489 | convolution fusion | flops 301989888 | bytes 17367040 | tf_op jit(solution)/shard_map/kmj,cmk->cmj/dot_general | solution.py:89
  804.7 19.0 %add_bitcast_fusion = (f32[6,32,512]{2,0,1:T(8,128)S(1)}, f32[6,32,512]{2,0,1:T(8,128)S(1)}) fusion(f32[32,512,6]{1,2,0:T(8,128)S(1)} %fusion.163, f32[32]{0:T(128)S(1)} %fusion.225, f32[6,32,256]{2,1,0:T(8,128)S(1)} %slice.203, f32[256,32,512]{2,1,0:T(8,128)S(1)} %bitcast.930), kind=kOutput, calls=%fused_computation.540 | convolution fusion | flops 302284800 | bytes 18153600 | tf_op jit(solution)/shard_map/kmj,cmk->cmj/dot_general | solution.py:86
  824.3 2.9 copy.76
  827.1 10.4 gather_fusion
  837.5 2.7 copy.77
  841.1 4.1 copy.78
  845.3 3.9 reshape.2533
  849.2 8.3 all-to-all-start
  857.6 1.9 multiply_reduce_fusion
  860.2 44.9 %psum.7 = f32[]{:T(128)} all-reduce(f32[]{:T(128)S(6)} %mul.6235), channel_id=1, replica_groups=mesh['band'=16,'shell'=2] {'band'}, use_global_device_ids=true, to_apply=%region_5.6 | all-reduce | flops 1 | bytes 8 | tf_op jit(solution)/shard_map/psum | solution.py:138
  905.7 3.6 reduce.1
  909.3 3.8 reshape.2534
  913.1 3.8 copy.79
  916.9 19.8 %fusion.174 = f32[3,64,2048]{2,1,0:T(8,128)S(1)} fusion(s32[512]{0:T(512)S(1)} %copy-done.4, f32[1,3,2,512,64]{4,3,2,1,0:T(8,128)} %bitcast.961), kind=kOutput, calls=%fused_computation.503 | convolution fusion | flops 2430599168 | bytes 2361344 | tf_op jit(solution)/shard_map/sfmr,mk->sfrk/dot_general | solution.py:128
  936.8 18.9 %fusion.189 = f32[1,3,64,2048]{3,2,1,0:T(8,128)S(1)} fusion(f32[3,64,2048]{2,1,0:T(8,128)S(1)} %fusion.174, s32[512]{0:T(512)S(1)} %copy-done.4, f32[1,3,2,512,64]{4,3,2,1,0:T(8,128)S(1)} %bitcast.962), kind=kOutput, calls=%fused_computation.514 | convolution fusion | flops 2431385600 | bytes 3934208 | tf_op jit(solution)/shard_map/sfmr,mk->sfrk/dot_general | solution.py:127
  956.5 19.8 %fusion.201 = f32[1,3,1,512,64]{3,4,1,2,0:T(8,128)S(1)} fusion(s32[512]{0:T(512)S(1)} %copy-done.4, f32[1,64,2048]{2,1,0:T(8,128)S(1)} %fusion.214, f32[1,64,2048]{2,1,0:T(8,128)S(1)} %get-tuple-element.827, f32[1,64,2048]{2,1,0:T(8,128)S(1)} %get-tuple-element.826, f32[64]{0:T(128)S(1)} %get-tuple-element.667), kind=kOutput, calls=%fused_computation.519 | convolution fusion | flops 2431778816 | bytes 1968384 | tf_op jit(solution)/shard_map/sfrk,mk->sfmr/dot_general | solution.py:147
  976.3 20.0 %fusion.198 = f32[1,3,1,512,64]{3,4,1,2,0:T(8,128)S(1)} fusion(s32[512]{0:T(512)S(1)} %copy-done.4, f32[1,64,2048]{2,1,0:T(8,128)S(1)} %fusion.214, f32[1,64,2048]{2,1,0:T(8,128)S(1)} %get-tuple-element.827, f32[1,64,2048]{2,1,0:T(8,128)S(1)} %get-tuple-element.826, f32[64]{0:T(128)S(1)} %get-tuple-element.667), kind=kOutput, calls=%fused_computation.518 | convolution fusion | flops 2431778816 | bytes 1968384 | tf_op jit(solution)/shard_map/sfrk,mk->sfmr/dot_general | solution.py:146
  997.5 2.6 reshape.2535
  1000.1 3.6 all-to-all-start.1
  1003.7 4.4 sort.17
  1008.1 9.0 all-to-all-done.1
  1017.1 2.5 reduce.2
  1020.9 3.4 copy.93
  1024.2 8.4 gather_fusion.1
  1032.7 3.4 copy.86
  1038.0 28.6 %fusion.207 = f32[6,32,256,1]{2,0,1,3:T(8,128)S(1)} fusion(f32[256,32,512]{2,1,0:T(8,128)} %bitcast.932, f32[6,32,512]{2,1,0:T(8,128)S(1)} %get-tuple-element.829), kind=kOutput, calls=%fused_computation.521 | convolution fusion | flops 301989888 | bytes 17367040 | tf_op jit(solution)/shard_map/kmj,cmj->cmk/dot_general | solution.py:98
  1066.6 28.3 %fusion.204 = f32[6,32,256,1]{2,0,1,3:T(8,128)S(1)} fusion(f32[256,32,512]{2,1,0:T(8,128)} %bitcast.929, f32[6,32,512]{2,1,0:T(8,128)S(1)} %get-tuple-element.828), kind=kOutput, calls=%fused_computation.520 | convolution fusion | flops 301989888 | bytes 17367040 | tf_op jit(solution)/shard_map/kmj,cmj->cmk/dot_general | solution.py:97
  (748 shorter events, 108.1 us)
Async XLA Ops:
  780.6 24.1 %copy-start = (f32[16,16,32,512]{3,2,1,0:T(8,128)S(1)}, f32[16,16,32,512]{3,2,1,0:T(8,128)}, u32[]{:S(2)}) copy-start(f32[16,16,32,512]{3,2,1,0:T(8,128)} %get-tuple-element.516) | copy-start | bytes 50331652
  841.1 16.4 %copy-start.3 = (s32[1024]{0:T(1024)S(1)}, s32[1024]{0:T(1024)}, u32[]{:S(2)}) copy-start(s32[1024]{0:T(1024)} %param.8) | copy-start | bytes 12292
  849.2 55.9 %all-to-all-start = ((f32[16,1,12288]{2,1,0:T(1,128)}), f32[16,1,12288]{2,1,0:T(1,128)S(1)}, u32[]{:S(2)}, u32[]{:S(2)}) async-start(f32[16,1,12288]{2,1,0:T(1,128)} %reshape.2533), calls=%async_computation | async-start | bytes 1572864 | tf_op jit(solution)/shard_map/all_to_all | solution.py:125
  909.3 7.6 copy-start.4
  916.9 19.8 %copy-start.2 = (f32[1,3,2,32,16,64]{5,3,4,2,1,0:T(8,128)S(1)}, f32[1,3,2,32,16,64]{5,3,4,2,1,0:T(8,128)}, u32[]{:S(2)}) copy-start(f32[1,3,2,32,16,64]{5,3,4,2,1,0:T(8,128)} %copy.79) | copy-start | bytes 2359300
  936.7 19.0 %copy-start.1 = (f32[1,64,2048]{2,1,0:T(8,128)S(1)}, f32[1,64,2048]{2,1,0:T(8,128)}, u32[]{:S(2)}) copy-start(f32[1,64,2048]{2,1,0:T(8,128)} %param.7) | copy-start | bytes 1572868
  1000.1 17.0 %all-to-all-start.1 = ((f32[16,1,12288]{2,1,0:T(1,128)}), f32[16,1,12288]{2,1,0:T(1,128)S(1)}, u32[]{:S(2)}, u32[]{:S(2)}) async-start(f32[16,1,12288]{2,1,0:T(1,128)} %reshape.2535), calls=%async_computation.1 | async-start | bytes 1572864 | tf_op jit(solution)/shard_map/all_to_all | solution.py:151
where the time goes:
time: 1110 us; the launch traced here: 1100 us
  loops' own time  663 us (60%)
  matrix products  178 us (16%)
  local copies, waits for them, and re-layouts  108 us (10%)
  other arithmetic  80.3 us (7%)
  blocking collectives  44.9 us (4%)
  starting transfers between devices  11.9 us (1%)
    another operation x1, loops' own time, legendre_halves(): lax.scan(two_degrees, (zeros_start, zeros_start, start_log), steps, unrol...  663 us
    while x368, other arithmetic  48.8 us
    psum x1, blocking collectives, per_device(): rate_mean = lax.psum(local_total, 'band')  44.9 us
    dot_general x1, matrix products, analyze(): jnp.einsum('kmj,cmj->cmk', odd_table, odd_data, precision=lax.Precision.H...  28.6 us
    dot_general x1, matrix products, analyze(): jnp.einsum('kmj,cmj->cmk', even_table, even_data, precision=lax.Precision...  28.3 us
    dynamic_update_slice x16, local copies, waits for them, and re-layouts, legendre_halves(): lax.scan(two_degrees, (zeros_start, zeros_start, start_log), steps, unrol...  26.3 us
    dot_general x1, matrix products, synthesize(): jnp.einsum('kmj,cmk->cmj', odd_table, coeffs[:, :, 1::2], precision=lax.P...  24.1 us
  transfers between devices with their start and end apart: 2, of which 1 were waited for; matrix products, arithmetic and copies ran while one was open for 1% of the time, Pallas kernels for 0%

commit v1 on v0

v1 whole, which is shorter than its diff:
```python
import math

import jax
import jax.numpy as jnp
import numpy as np
from jax import lax
from jax.experimental import pallas as pl
from jax.experimental.pallas import tpu as pltpu
from jax.sharding import PartitionSpec as P

DEG = 512
NLAT = 1024
NLON = 2048
FIELDS = 3
HALF = NLAT // 2
CHAN = 2 * FIELDS
BLK = 8
ROWS = CHAN * BLK
CHUNK = 64
LANES = 128
KTILE = 256
BF = jnp.bfloat16
F32 = jnp.float32


def split_two(value):
    high = value.astype(BF)
    low = (value - high.astype(F32)).astype(BF)
    return high, low


def dot(lhs, rhs, contract_rhs=0):
    return lax.dot_general(
        lhs, rhs, (((1,), (contract_rhs,)), ((), ())), preferred_element_type=F32
    )


def latitude_rows():
    theta = np.pi * (np.arange(HALF) + 0.5) / NLAT
    index = np.arange(DEG, dtype=np.float64)
    log_terms = np.zeros(DEG)
    log_terms[1:] = 0.5 * np.log2((2.0 * index[1:] + 1.0) / (2.0 * index[1:]))
    rows = np.zeros((8, DEG))
    rows[0], rows[1], rows[2] = np.cos(theta), np.log2(np.sin(theta)), log_terms
    return rows.astype(np.float32)


def spread_matrix():
    spread = np.zeros((LANES, 2, 2, CHUNK // 2, BLK), np.float32)
    for half in range(2):
        for parity in range(2):
            for step in range(CHUNK // 2):
                spread[half * CHUNK + 2 * step + parity, half, parity, step, :] = 1.0
    return spread.reshape(LANES, 2 * 2 * (CHUNK // 2) * BLK).astype(BF)


def block_orders(slots_ref, first):
    sublane = lax.broadcasted_iota(jnp.int32, (BLK, LANES), 0)
    orders = jnp.zeros((BLK, LANES), jnp.int32)
    lowest = jnp.int32(DEG)
    for i in range(BLK):
        order = slots_ref[first + i]
        orders = jnp.where(sublane == i, order, orders)
        lowest = jnp.minimum(lowest, order)
    return orders[:, :1], lowest


def recursion_tables(order, rows_ref, alpha_ref, beta_ref):
    degree = lax.broadcasted_iota(jnp.int32, (BLK, DEG), 1).astype(F32)
    order_sq = order * order
    denominator = degree * degree - order_sq
    safe = jnp.where(denominator > 0, denominator, 1.0)
    alpha = jnp.sqrt((4.0 * degree * degree - 1.0) / safe)
    back = jnp.maximum((degree - 1.0) * (degree - 1.0) - order_sq, 0.0)
    beta = jnp.sqrt(back * (2.0 * degree + 1.0) / (safe * jnp.maximum(2.0 * degree - 3.0, 1.0)))
    alpha_ref[...] = jnp.where(degree > order, alpha, 0.0)
    beta_ref[...] = jnp.where(degree > order, beta, -1.0)
    terms = jnp.where(degree <= order, rows_ref[2:3, :], 0.0)
    norm = jnp.where(order > 0, 0.5 + jnp.sum(terms, axis=1, keepdims=True), 0.0)
    return norm + order * rows_ref[1:2, :]


def run_chunk(step, carry, cosine, alpha_ref, beta_ref, emit):
    current, previous, log_scale = carry
    tile = pl.ds(pl.multiple_of(step // 2 * LANES, LANES), LANES)
    shift = (step % 2) * CHUNK
    alpha = pltpu.roll(alpha_ref[:, tile], shift, 1)
    beta = pltpu.roll(beta_ref[:, tile], shift, 1)
    scale = None
    for i in range(CHUNK):
        if i % 16 == 0:
            large = jnp.abs(current) > 2.0**60
            factor = jnp.where(large, 2.0**-60, 1.0)
            current = current * factor
            previous = previous * factor
            log_scale = jnp.where(large, log_scale + 60.0, log_scale)
            scale = jnp.exp2(jnp.maximum(log_scale, -200.0))
        newest = (alpha[:, i : i + 1] * cosine) * current - beta[:, i : i + 1] * previous
        current, previous = newest, current
        emit(i, newest * scale)
    return current, previous, log_scale


def start_state(log_start):
    ones = jnp.ones((BLK, HALF), F32)
    return ones, ones, log_start


def fold_matrix(latitude_ref, fold_ref):
    latitude = latitude_ref[...]
    north = jnp.where(latitude < HALF, latitude, NLAT - 1 - latitude)
    sublane = lax.broadcasted_iota(jnp.int32, (HALF, NLAT), 0)
    fold_ref[...] = jnp.where(sublane == north, 1.0, 0.0).astype(BF)


def synth_kernel(
    dims, slots_ref, spec_ref, rows_ref, spread_ref, latitude_ref, out_ref,
    alpha_ref, beta_ref, lhs_ref, high_ref, low_ref, acc_ref, fold_ref,
):
    bands, row_count, modes, first_block, blocks, tiles = dims
    fold_matrix(latitude_ref, fold_ref)
    base = lax.axis_index("band") * modes + first_block * BLK
    south = latitude_ref[...] >= HALF
    spread_width = 4 * (CHUNK // 2) * BLK
    lane = lax.broadcasted_iota(jnp.int32, (2 * ROWS, spread_width), 1)
    sub = lax.broadcasted_iota(jnp.int32, (2 * ROWS, spread_width), 0)
    diagonal = (lane % BLK) == (sub % BLK)
    width = (CHUNK // 2) * BLK

    def one_block(block, unused):
        orders, lowest = block_orders(slots_ref, base + block * BLK)
        order = orders.astype(F32)
        log_start = recursion_tables(order, rows_ref, alpha_ref, beta_ref)
        here = pl.ds(pl.multiple_of(block * BLK, BLK), BLK)
        degree = lax.broadcasted_iota(jnp.int32, (BLK, DEG), 1)
        coeffs = jnp.where((degree >= orders)[None], spec_ref[:, here, :], 0.0)
        coeff_high, coeff_low = split_two(coeffs.reshape(ROWS, DEG))
        stacked = jnp.concatenate([coeff_high, coeff_low], 0)
        for t in range(DEG // LANES):
            wide = dot(stacked[:, t * LANES : (t + 1) * LANES], spread_ref[...])
            wide = jnp.where(diagonal, wide, 0.0).astype(BF)
            for half in range(2):
                lhs_ref[2 * t + half] = wide[:, half * 2 * width : (half + 1) * 2 * width]
        acc_ref[...] = jnp.zeros_like(acc_ref)
        cosine = jnp.broadcast_to(rows_ref[0:1, :], (BLK, HALF))

        def one_chunk(step, carry):
            held = {}

            def emit(i, value):
                if i % 4 < 2:
                    held[i] = value
                else:
                    pair = jnp.concatenate([held.pop(i - 2), value], 0)
                    high, low = split_two(pair)
                    at = (i // 4) * 2 * BLK
                    high_ref[i % 2, at : at + 2 * BLK, :] = high
                    low_ref[i % 2, at : at + 2 * BLK, :] = low

            carry = run_chunk(step, carry, cosine, alpha_ref, beta_ref, emit)
            for parity in range(2):
                lhs = lhs_ref[step, :, parity * width : (parity + 1) * width]
                first = dot(lhs, high_ref[parity])
                second = dot(lhs[:ROWS], low_ref[parity])
                acc_ref[parity] += first[:ROWS] + first[ROWS:] + second
            return carry

        lax.fori_loop(lowest // CHUNK, DEG // CHUNK, one_chunk, start_state(log_start))
        both = acc_ref[...].reshape(2 * ROWS, HALF)
        high, low = split_two(both)
        moved = dot(jnp.concatenate([high, low], 0), fold_ref[...])
        moved = moved[: 2 * ROWS] + moved[2 * ROWS :]
        sign = jnp.tile(1.0 - 2.0 * (orders % 2).astype(F32), (CHAN, 1))
        even, odd = moved[:ROWS], moved[ROWS:]
        values = jnp.where(south, sign * (even - odd), even + odd)
        for d in range(bands):
            parts = []
            for kind in range(2):
                for field in range(FIELDS):
                    c = field * 2 + kind
                    parts.append(
                        values[c * BLK : (c + 1) * BLK, d * row_count : (d + 1) * row_count]
                    )
            if CHAN * row_count < tiles * LANES:
                parts.append(jnp.zeros((BLK, tiles * LANES - CHAN * row_count), F32))
            joined = jnp.concatenate(parts, 1)
            for t in range(tiles):
                at = pl.ds(pl.multiple_of(t * blocks * BLK + block * BLK, BLK), BLK)
                out_ref[d, at, :] = joined[:, t * LANES : (t + 1) * LANES]
        return unused

    lax.fori_loop(0, blocks, one_block, 0)


def analyze_kernel(
    dims, slots_ref, data_ref, total_ref, rows_ref, latitude_ref, out_ref,
    alpha_ref, beta_ref, high_ref, low_ref, weight_ref, result_ref, fold_ref,
):
    bands, row_count, modes, first_block, blocks, tiles = dims
    fold_matrix(latitude_ref, fold_ref)
    base = lax.axis_index("band") * modes + first_block * BLK
    south = latitude_ref[...] >= HALF
    total = total_ref[0]
    for d in range(1, bands):
        total = total + total_ref[d]
    inverse = (1.0 / total)[:, :1]
    lane = lax.broadcasted_iota(jnp.int32, (CHUNK * BLK, LANES), 1)
    sub = lax.broadcasted_iota(jnp.int32, (CHUNK * BLK, LANES), 0)
    keep = (lane % BLK == sub % BLK) & (lane // ROWS == sub // BLK % 2)

    def one_block(block, unused):
        orders, lowest = block_orders(slots_ref, base + block * BLK)
        order = orders.astype(F32)
        log_start = recursion_tables(order, rows_ref, alpha_ref, beta_ref)
        sign = 1.0 - 2.0 * (orders % 2).astype(F32)
        evens, odds = [], []
        for c in range(CHAN):
            offset = ((c % 2) * FIELDS + c // 2) * row_count
            t, at = offset // LANES, offset % LANES
            rows = pl.ds(pl.multiple_of(t * blocks * BLK + block * BLK, BLK), BLK)
            values = jnp.concatenate(
                [data_ref[d, rows, :][:, at : at + row_count] for d in range(bands)], 1
            )
            flipped = sign * values
            evens.append(jnp.where(south, flipped, values))
            odds.append(jnp.where(south, -flipped, values))
        high, low = split_two(jnp.concatenate(evens + odds, 0))
        folded = dot(jnp.concatenate([high, low], 0), fold_ref[...], 1)
        folded = folded[: 2 * ROWS] + folded[2 * ROWS :]
        padded = jnp.concatenate([folded, jnp.zeros((LANES - 2 * ROWS, HALF), F32)], 0)
        high, low = split_two(padded.T)
        weight_ref[:, :LANES] = high
        weight_ref[:, LANES:] = low
        result_ref[...] = jnp.zeros_like(result_ref)
        cosine = jnp.broadcast_to(rows_ref[0:1, :], (BLK, HALF))

        def one_chunk(step, carry):
            held = {}

            def emit(i, value):
                if i % 2 == 0:
                    held[i] = value
                else:
                    pair = jnp.concatenate([held.pop(i - 1), value], 0)
                    high, low = split_two(pair)
                    at = (i // 2) * 2 * BLK
                    high_ref[at : at + 2 * BLK, :] = high
                    low_ref[at : at + 2 * BLK, :] = low

            carry = run_chunk(step, carry, cosine, alpha_ref, beta_ref, emit)
            first = dot(high_ref[...], weight_ref[...])
            second = dot(low_ref[...], weight_ref[:, :LANES])
            full = first[:, :LANES] + first[:, LANES:] + second
            picked = jnp.where(keep, full, 0.0).reshape(CHUNK, BLK, LANES)
            at = pl.ds(pl.multiple_of(step * CHUNK, CHUNK), CHUNK)
            result_ref[at, :] = jnp.sum(picked, axis=1)
            return carry

        lax.fori_loop(lowest // CHUNK, DEG // CHUNK, one_chunk, start_state(log_start))
        turned = result_ref[...].T
        turned = turned[:ROWS] + turned[ROWS : 2 * ROWS]
        degree = lax.broadcasted_iota(jnp.int32, (BLK, DEG), 1)
        here = pl.ds(pl.multiple_of(block * BLK, BLK), BLK)
        for c in range(CHAN):
            part = jnp.where(degree >= orders, turned[c * BLK : (c + 1) * BLK], 0.0)
            if c // 2 == FIELDS - 1:
                part = part * inverse
            out_ref[c, here, :] = part
        return unused

    lax.fori_loop(0, blocks, one_block, 0)


def base_trig(order, first):
    lane = lax.broadcasted_iota(jnp.int32, order.shape, 1) + first
    phase = (order * lane) & (NLON - 1)
    quarter = (phase + NLON // 8) >> 9
    rest = (phase - quarter * (NLON // 4)).astype(F32) * (2.0 * math.pi / NLON)
    square = rest * rest
    sine = 1.0 / 362880.0
    for coef in (-1.0 / 5040.0, 1.0 / 120.0, -1.0 / 6.0, 1.0):
        sine = sine * square + coef
    sine = sine * rest
    cosine = 1.0 / 40320.0
    for coef in (-1.0 / 720.0, 1.0 / 24.0, -0.5, 1.0):
        cosine = cosine * square + coef
    swap = (quarter & 1) == 1
    cos_out = jnp.where(swap, sine, cosine)
    sin_out = jnp.where(swap, cosine, sine)
    cos_out = jnp.where(((quarter + 1) & 2) == 2, -cos_out, cos_out)
    sin_out = jnp.where((quarter & 2) == 2, -sin_out, sin_out)
    return cos_out, sin_out


def grid_kernel(
    dims, *refs,
):
    bands, row_count, modes, pieces, tiles, slots = dims
    data_refs = refs[:pieces]
    orders_ref, rate_ref, sine_ref = refs[pieces : pieces + 3]
    out_refs = refs[pieces + 3 : 2 * pieces + 3]
    total_ref = refs[2 * pieces + 3]
    (lhs_ref, cos_ref, sin_ref, turn_cos, turn_sin, high_ref, low_ref, weight_ref, acc_ref) = refs[
        2 * pieces + 4 :
    ]
    piece_modes = modes // pieces
    piece_slots = bands * piece_modes
    group = FIELDS * row_count
    padded = weight_ref.shape[0] // 2

    for p in range(pieces):
        columns = []
        for t in range(tiles):
            part = data_refs[p][:, t * piece_modes : (t + 1) * piece_modes, :]
            columns.append(part.reshape(piece_slots, LANES).T)
        turned = jnp.concatenate(columns, 0)
        for kind in range(2):
            high, low = split_two(turned[kind * group : (kind + 1) * group])
            at = kind * slots + p * piece_slots
            lhs_ref[:group, at : at + piece_slots] = high
            lhs_ref[group:, at : at + piece_slots] = low

    def prepare(step, unused):
        at = pl.ds(pl.multiple_of(step * 64, 64), 64)
        order = orders_ref[at, :]
        for t in range(KTILE // LANES):
            cosine, sine = base_trig(order, t * LANES)
            cos_ref[at, t * LANES : (t + 1) * LANES] = cosine
            sin_ref[at, t * LANES : (t + 1) * LANES] = sine
        eighth = order & 7
        root = math.sqrt(0.5)
        odd = (eighth & 1) == 1
        turned_cos = jnp.where(odd, root, jnp.where((eighth & 2) == 0, 1.0, 0.0))
        turned_sin = jnp.where(odd, root, jnp.where((eighth & 2) == 2, 1.0, 0.0))
        turn_cos[at, :] = jnp.where((eighth >= 3) & (eighth <= 5), -turned_cos, turned_cos)
        turn_sin[at, :] = jnp.where(eighth > 4, -turned_sin, turned_sin)
        return unused

    lax.fori_loop(0, slots // 64, prepare, 0)
    acc_ref[...] = jnp.zeros_like(acc_ref)
    weight_ref[...] = jnp.zeros_like(weight_ref)
    flux_scale = math.pi / (2.0 * NLAT * NLON * DEG)

    def one_tile(step, total):
        for s in range(0, slots, 64):
            rows_at = slice(s, s + 64)
            more_cos = jnp.tile(turn_cos[rows_at, :], (1, KTILE // LANES))
            more_sin = jnp.tile(turn_sin[rows_at, :], (1, KTILE // LANES))
            cosine, sine = cos_ref[rows_at, :], sin_ref[rows_at, :]
            cos_ref[rows_at, :] = cosine * more_cos - sine * more_sin
            sin_ref[rows_at, :] = sine * more_cos + cosine * more_sin
            high, low = split_two(cosine)
            high_ref[rows_at, :], low_ref[rows_at, :] = high, low
            high, low = split_two(sine)
            high_ref[slots + s : slots + s + 64, :] = high
            low_ref[slots + s : slots + s + 64, :] = low
        first = dot(lhs_ref[...], high_ref[...])
        second = dot(lhs_ref[:group, :], low_ref[...])
        fields = first[:group] + first[group:] + second
        weight = jnp.tile(sine_ref[...], (1, KTILE // LANES))
        columns = pl.ds(pl.multiple_of(step * KTILE, KTILE), KTILE)
        weighted_rate = rate_ref[:, columns] * weight
        scaled = fields[:row_count] * (weight * flux_scale)
        values = jnp.concatenate(
            [
                fields[row_count : 2 * row_count] * scaled,
                fields[2 * row_count :] * scaled,
                weighted_rate * fields[:row_count],
            ],
            0,
        )
        high, low = split_two(values)
        weight_ref[:group, :] = high
        weight_ref[padded : padded + group, :] = low
        first = dot(high_ref[...], weight_ref[...], 1)
        second = dot(low_ref[...], weight_ref[:padded, :], 1)
        acc_ref[...] += first[:, :padded] + first[:, padded:] + second
        return total + jnp.sum(weighted_rate.reshape(row_count // 8, 8, KTILE), axis=0)

    total = lax.fori_loop(0, NLON // KTILE, one_tile, jnp.zeros((8, KTILE), F32))
    total_ref[...] = jnp.broadcast_to(jnp.sum(total), (bands, 8, LANES))
    for p in range(pieces):
        at = p * piece_slots
        joined = [
            acc_ref[at : at + piece_slots, :group],
            acc_ref[slots + at : slots + at + piece_slots, :group],
        ]
        if 2 * group < tiles * LANES:
            joined.append(jnp.zeros((piece_slots, tiles * LANES - 2 * group), F32))
        joined = jnp.concatenate(joined, 1)
        for t in range(tiles):
            part = joined[:, t * LANES : (t + 1) * LANES]
            out_refs[p][:, t * piece_modes : (t + 1) * piece_modes, :] = part.reshape(
                bands, piece_modes, LANES
            )


VMEM = pl.BlockSpec(memory_space=pltpu.VMEM)
SMEM = pl.BlockSpec(memory_space=pltpu.SMEM)
PIECES = 1


def per_device(spectrum, capture_rate, row_latitude, slot_wavenumber):
    bands = lax.axis_size("band")
    modes = spectrum.shape[3]
    row_count = capture_rate.shape[1]
    slots = slot_wavenumber.shape[0]
    blocks = modes // BLK
    pieces = min(PIECES, blocks)
    per_piece = blocks // pieces
    tiles = -(-CHAN * row_count // LANES)
    band_index = lax.axis_index("band")
    rows = jnp.asarray(latitude_rows())
    spread = jnp.asarray(spread_matrix())
    latitude = row_latitude.reshape(1, NLAT)
    coeffs = spectrum.reshape(CHAN, modes, DEG)
    params = pltpu.CompilerParams(vmem_limit_bytes=48 * 2**20)
    chunk_rows = tiles * per_piece * BLK

    def synth(p):
        dims = (bands, row_count, modes, p * per_piece, per_piece, tiles)
        return pl.pallas_call(
            lambda *refs: synth_kernel(dims, *refs),
            out_shape=jax.ShapeDtypeStruct((bands, chunk_rows, LANES), F32),
            in_specs=[SMEM, VMEM, VMEM, VMEM, VMEM],
            out_specs=VMEM,
            scratch_shapes=[
                pltpu.VMEM((BLK, DEG), F32),
                pltpu.VMEM((BLK, DEG), F32),
                pltpu.VMEM((DEG // CHUNK, 2 * ROWS, CHUNK * BLK), BF),
                pltpu.VMEM((2, CHUNK // 2 * BLK, HALF), BF),
                pltpu.VMEM((2, CHUNK // 2 * BLK, HALF), BF),
                pltpu.VMEM((2, ROWS, HALF), F32),
                pltpu.VMEM((HALF, NLAT), BF),
            ],
            compiler_params=params,
            name="synth",
        )(
            slot_wavenumber,
            coeffs[:, p * per_piece * BLK : (p + 1) * per_piece * BLK],
            rows, spread, latitude,
        )

    def analyze(p, data, total):
        dims = (bands, row_count, modes, p * per_piece, per_piece, tiles)
        return pl.pallas_call(
            lambda *refs: analyze_kernel(dims, *refs),
            out_shape=jax.ShapeDtypeStruct((CHAN, per_piece * BLK, DEG), F32),
            in_specs=[SMEM, VMEM, VMEM, VMEM, VMEM],
            out_specs=VMEM,
            scratch_shapes=[
                pltpu.VMEM((BLK, DEG), F32),
                pltpu.VMEM((BLK, DEG), F32),
                pltpu.VMEM((CHUNK * BLK, HALF), BF),
                pltpu.VMEM((CHUNK * BLK, HALF), BF),
                pltpu.VMEM((HALF, 2 * LANES), BF),
                pltpu.VMEM((DEG, LANES), F32),
                pltpu.VMEM((HALF, NLAT), BF),
            ],
            compiler_params=params,
            name="analyze",
        )(slot_wavenumber, data, total, rows, latitude)

    def exchange(value):
        return lax.all_to_all(value, "band", split_axis=0, concat_axis=0, tiled=True)

    received = [exchange(synth(p)) for p in range(pieces)]

    my_latitudes = lax.dynamic_slice_in_dim(row_latitude, band_index * row_count, row_count)
    row_sine = jnp.sin(jnp.pi * (my_latitudes.astype(F32) + 0.5) / NLAT)
    row_sine = jnp.broadcast_to(row_sine[:, None], (row_count, LANES))
    orders = slot_wavenumber.reshape(bands, pieces, per_piece * BLK).transpose(1, 0, 2)
    orders = jnp.broadcast_to(orders.reshape(slots, 1), (slots, LANES))
    group = FIELDS * row_count
    padded = -(-group // LANES) * LANES
    dims = (bands, row_count, modes, pieces, tiles, slots)
    outs = pl.pallas_call(
        lambda *refs: grid_kernel(dims, *refs),
        out_shape=[jax.ShapeDtypeStruct((bands, chunk_rows, LANES), F32)] * pieces
        + [jax.ShapeDtypeStruct((bands, 8, LANES), F32)],
        in_specs=[VMEM] * (pieces + 3),
        out_specs=[VMEM] * (pieces + 1),
        scratch_shapes=[
            pltpu.VMEM((2 * group, 2 * slots), BF),
            pltpu.VMEM((slots, KTILE), F32),
            pltpu.VMEM((slots, KTILE), F32),
            pltpu.VMEM((slots, LANES), F32),
            pltpu.VMEM((slots, LANES), F32),
            pltpu.VMEM((2 * slots, KTILE), BF),
            pltpu.VMEM((2 * slots, KTILE), BF),
            pltpu.VMEM((2 * padded, KTILE), BF),
            pltpu.VMEM((2 * slots, padded), F32),
        ],
        compiler_params=params,
        name="grid",
    )(*received, orders, capture_rate.reshape(row_count, NLON), row_sine)
    total = exchange(outs[pieces])
    parts = [analyze(p, exchange(outs[p]), total) for p in range(pieces)]
    result = parts[0] if pieces == 1 else jnp.concatenate(parts, 1)
    return result.reshape(1, FIELDS, 2, modes, DEG)


def solution(mesh):
    return jax.shard_map(
        per_device,
        mesh=mesh,
        in_specs=(P("shell", None, None, "band", None), P("shell", "band", None), P(), P()),
        out_specs=P("shell", None, None, "band", None),
        check_vma=False,
    )
```

time: 1110 us -> 130 us (0.12); the launches traced: 1100 us -> 129 us
  loops' own time: 663 us -> 0 us
  matrix products: 178 us -> 0 us
  local copies, waits for them, and re-layouts: 108 us -> 4.91 us
  other arithmetic: 80.3 us -> 0.11 us
  Pallas kernels: 0 us -> 61.5 us
    another operation x1 -> x0, loops' own time: 663 us -> none  [legendre_halves(): lax.scan(two_degrees, (zeros_start, zeros_start, start_log), steps, unrol...]
    dot_general x8 -> x0, matrix products: 178 us -> none  [the longest x1 28.6 us: analyze(): jnp.einsum('kmj,cmj->cmk', odd_table, odd_data, precision=lax.Precision.H...]
    pallas_call x0 -> x3, Pallas kernels: none -> 61.5 us  [the longest x1 23.7 us: analyze(): pl.pallas_call(lambda *refs: analyze_kernel(dims, *refs), out_shape=jax.S...]
    while x368 -> x0, other arithmetic: 48.8 us -> none
    psum x1 -> x0, blocking collectives: 44.9 us -> none  [per_device(): rate_mean = lax.psum(local_total, 'band')]
    all_to_all x0 -> x2, blocking collectives: none -> 34 us  [exchange(): lax.all_to_all(value, 'band', split_axis=0, concat_axis=0, tiled=True)]
    slice x19 -> x0, local copies, waits for them, and re-layouts: 26.6 us -> none  [the longest x16 11.5 us: legendre_halves(): lax.scan(two_degrees, (zeros_start, zeros_start, start_log), steps, unrol...]
    dynamic_update_slice x16 -> x0, local copies, waits for them, and re-layouts: 26.3 us -> none  [legendre_halves(): lax.scan(two_degrees, (zeros_start, zeros_start, start_log), steps, unrol...]
  transfers between devices with their start and end apart: 2 -> 1, of which waited for: 1 -> 1; matrix products, arithmetic and copies ran while one was open for 1% -> 0% of each run, Pallas kernels for 0% -> 0%
where the time goes in v1:
time: 130 us; the launch traced here: 129 us
  Pallas kernels  61.5 us (47%)
  blocking collectives  34 us (26%)
  waiting for transfers between devices  18.9 us (15%)
  starting transfers between devices  9.4 us (7%)
  local copies, waits for them, and re-layouts  4.91 us (4%)
    all_to_all x2, blocking collectives, exchange(): lax.all_to_all(value, 'band', split_axis=0, concat_axis=0, tiled=True)  34 us
    pallas_call x1, Pallas kernels, analyze(): pl.pallas_call(lambda *refs: analyze_kernel(dims, *refs), out_shape=jax.S...  23.7 us
    pallas_call x1, Pallas kernels, synth(): pl.pallas_call(lambda *refs: synth_kernel(dims, *refs), out_shape=jax.Sha...  23.4 us
    all_to_all x1, waiting for transfers between devices, exchange(): lax.all_to_all(value, 'band', split_axis=0, concat_axis=0, tiled=True)  18.9 us
    pallas_call x1, Pallas kernels, per_device(): pl.pallas_call(lambda *refs: grid_kernel(dims, *refs), out_shape=[jax.Sha...  14.4 us
    all_to_all x1, starting transfers between devices, exchange(): lax.all_to_all(value, 'band', split_axis=0, concat_axis=0, tiled=True)  9.4 us
    unnamed x16, local copies, waits for them, and re-layouts  4.72 us
  transfers between devices with their start and end apart: 1, of which 1 were waited for; matrix products, arithmetic and copies ran while one was open for 0% of the time, Pallas kernels for 0%

profile of v1, /device:TPU:0, one launch (start us, length us, event | category | flops | bytes accessed | tf_op | source)
XLA Modules:
  0.0 128.9 jit_solution(4179497660558704266)
XLA Ops:
  0.0 0.0 copy-start.5
  0.0 0.7 copy-done.5
  0.7 0.0 copy-start.1
  0.7 1.0 copy-done.1
  1.7 0.0 copy-start.2
  1.7 0.9 copy-done.2
  2.6 0.0 copy-start.3
  2.6 0.7 copy-done.3
  3.3 0.0 copy-start.6
  3.3 0.7 copy-done.6
  4.0 23.4 %synth.1 = f32[16,96,128]{2,1,0:T(8,128)} custom-call(s32[512]{0:T(512)S(1)} %copy-done.5, f32[6,32,512]{2,1,0:T(8,128)S(1)} %bitcast.5, f32[8,512]{1,0:T(8,128)S(1)} %copy-done.3, bf16[128,1024]{1,0:T(8,128)(2,1)S(1)} %copy-done.2, s32[1,1024]{1,0:T(1,128)S(1)} %bitcast.6), custom_call_target="tpu_custom_call" | custom-call | tf_op jit(solution)/shard_map/synth/pallas_call | solution.py:422
  27.5 0.0 copy-start
  27.5 9.4 %all-to-all-start = ((f32[16,96,128]{2,1,0:T(8,128)}), f32[16,96,128]{2,1,0:T(8,128)S(1)}, u32[]{:S(2)}, u32[]{:S(2)}) async-start(f32[16,96,128]{2,1,0:T(8,128)} %synth.1), calls=%async_computation | async-start | bytes 1572864 | tf_op jit(solution)/shard_map/all_to_all | solution.py:465
  36.9 0.0 copy-start.7
  36.9 0.7 copy-done.7
  37.6 0.1 multiply_sine_fusion
  37.7 18.9 %all-to-all-done.refs_0_ = f32[16,96,128]{2,1,0:T(8,128)S(1)} async-done(((f32[16,96,128]{2,1,0:T(8,128)}), f32[16,96,128]{2,1,0:T(8,128)S(1)}, u32[]{:S(2)}, u32[]{:S(2)}) %all-to-all-start) | async-done | bytes 786464 | tf_op jit(solution)/shard_map/all_to_all | solution.py:465
  56.6 0.1 broadcast_in_dim.5.refs_3_
  56.7 0.1 broadcast_in_dim.4.refs_1_
  56.8 0.0 copy-done
  56.8 14.4 %grid.1 = (f32[16,96,128]{2,1,0:T(8,128)S(1)}, f32[16,8,128]{2,1,0:T(8,128)S(1)}) custom-call(f32[16,96,128]{2,1,0:T(8,128)S(1)} %all-to-all-done.refs_0_, s32[512,128]{1,0:T(8,128)S(1)} %broadcast_in_dim.4.refs_1_, f32[64,2048]{1,0:T(8,128)S(1)} %bitcast.4, f32[64,128]{1,0:T(8,128)S(1)} %broadcast_in_dim.5.refs_3_), custom_call_target="tpu_custom_call" | custom-call | tf_op jit(solution)/shard_map/grid/pallas_call | solution.py:477
  71.3 12.2 %all_to_all.15.refs_2_ = f32[16,8,128]{2,1,0:T(8,128)S(1)} all-to-all(f32[16,8,128]{2,1,0:T(8,128)S(1)} %get-tuple-element.8), channel_id=1, replica_groups=mesh['band'=16,'shell'=2] {'band'}, dimensions={0} | all-to-all | bytes 131072 | tf_op jit(solution)/shard_map/all_to_all | solution.py:465
  83.5 0.0 copy-start.4
  83.5 21.8 %all_to_all.16.refs_1_ = f32[16,96,128]{2,1,0:T(8,128)S(1)} all-to-all(f32[16,96,128]{2,1,0:T(8,128)S(1)} %get-tuple-element.7), channel_id=1, replica_groups=mesh['band'=16,'shell'=2] {'band'}, dimensions={0} | all-to-all | bytes 1572864 | tf_op jit(solution)/shard_map/all_to_all | solution.py:465
  105.2 0.0 copy-done.4
  105.3 23.7 %analyze.1 = f32[6,32,512]{2,1,0:T(8,128)} custom-call(s32[512]{0:T(512)S(1)} %copy-done.5, f32[16,96,128]{2,1,0:T(8,128)S(1)} %all_to_all.16.refs_1_, f32[16,8,128]{2,1,0:T(8,128)S(1)} %all_to_all.15.refs_2_, f32[8,512]{1,0:T(8,128)S(1)} %copy-done.4, s32[1,1024]{1,0:T(1,128)S(1)} %bitcast.7), custom_call_target="tpu_custom_call" | custom-call | tf_op jit(solution)/shard_map/analyze/pallas_call | solution.py:446
Async XLA Ops:
  0.0 0.7 copy-start.5
  0.7 1.0 copy-start.1
  1.7 0.9 copy-start.2
  2.6 0.7 copy-start.3
  3.3 0.7 copy-start.6
  27.5 29.4 %copy-start = (f32[1,64,2048]{2,1,0:T(8,128)S(1)}, f32[1,64,2048]{2,1,0:T(8,128)}, u32[]{:S(2)}) copy-start(f32[1,64,2048]{2,1,0:T(8,128)} %param.7) | copy-start | bytes 1572868
  27.5 29.2 %all-to-all-start = ((f32[16,96,128]{2,1,0:T(8,128)}), f32[16,96,128]{2,1,0:T(8,128)S(1)}, u32[]{:S(2)}, u32[]{:S(2)}) async-start(f32[16,96,128]{2,1,0:T(8,128)} %synth.1), calls=%async_computation | async-start | bytes 1572864 | tf_op jit(solution)/shard_map/all_to_all | solution.py:465
  36.9 0.7 copy-start.7
  83.5 21.8 %copy-start.4 = (f32[8,512]{1,0:T(8,128)S(1)}, f32[8,512]{1,0:T(8,128)}, u32[]{:S(2)}) copy-start(f32[8,512]{1,0:T(8,128)} %constant.23.clone.refs_2_.refs_3_) | copy-start | bytes 49156
